TPU v7x, 32 devices: a whole 2x2x4 slice. The times are simulated.
32 devices in a mesh: groups: 2 (over y), row: 4 (over x, core), col: 4 (over z).
Axes of the slice: x: 2, y: 2, z: 4, core: 2. Of those that a mesh axis runs over, the one named last changes fastest.
Arguments:
- trial_panel: bfloat16 [8, 4, 512, 256], P(('groups', 'col'), 'row'), parts along dimension 0, may hold values from -6 to 6
- tile_values: bfloat16 [8, 4, 128, 128, 128], P(('groups', 'row'), 'col'), parts along dimension 0, as said below
- tile_rows: int32 [8, 4, 128], P(('groups', 'row'), 'col'), parts along dimension 0, may hold values from 0 to 15, as said below
- tile_cols: int32 [8, 4, 128], P(('groups', 'row'), 'col'), parts along dimension 0, may hold values from 0 to 15, as said below
- tile_counts: int32 [8, 4], P(('groups', 'row'), 'col'), parts along dimension 0, may hold values from 32 to 128, as said below
Outputs:
- filtered_panel: float32 [8, 4, 512, 256], P(('groups', 'row'), 'col'), parts along dimension 0
There are 2 independent parts, one for each index of `groups`. A program takes and returns all parts, laid end to end along the dimension named above; each array names one. Nothing has to cross between parts.
Inputs may be any that keep to these rules, and one draw needn't show every extreme that they name: `tile_rows`: cell (c, r) lists in each slot the tile of the same slot of cell (r, c) mirrored (rows and columns swapped); on a cell with r == c slot s + 64 mirrors slot s. Within a cell the slots name distinct positions (block row, block column), except that on a cell with r == c slots s and s + 64 share a position when it lies on the diagonal. `tile_cols`: mirrored as tile_rows is. `tile_counts`: the used slots are the first ones; cells (r, c) and (c, r) use equally many; cells with r == c use all 128. `tile_values`: the tile of a slot of cell (c, r) is the transpose of the tile of the same slot of cell (r, c); on a cell with r == c the tile of slot s + 64 is the transpose of that of slot s.
All inputs are finite; a program needn't handle non-finite values.
Results may differ from a plain program's by a relative error of at most 0.02.
Values may be sent and summed in bfloat16 or wider, within the bound.
A program may use at most 64 MiB of HBM per device.

v0:
```python
import jax
import jax.numpy as jnp
from jax import lax
from jax.sharding import PartitionSpec as P

DEGREE = 3


filter_center = 0.5
filter_radius = 1.5


def cell_product(cell_tiles, rows_index, cols_index, used_count, source, flipped, on_diagonal):
    slot_total = cell_tiles.shape[0]
    block_total = source.shape[0]
    pick_index = rows_index if flipped else cols_index
    put_index = cols_index if flipped else rows_index
    einsum_form = "sba,sbw->saw" if flipped else "sab,sbw->saw"
    picked = jnp.take(source, pick_index, axis=0)
    products = jnp.einsum(
        einsum_form, cell_tiles, picked, preferred_element_type=jnp.float32
    ).astype(jnp.bfloat16)
    active = lax.iota(jnp.int32, slot_total) < used_count
    placing = (
        (put_index[None, :] == lax.iota(jnp.int32, block_total)[:, None]) & active[None, :]
    ).astype(jnp.bfloat16)
    summed = jnp.einsum("gs,saw->gaw", placing, products, preferred_element_type=jnp.float32)
    return summed - filter_center * on_diagonal * source.astype(jnp.float32)


def gather_grid_column(piece):
    return lax.all_gather(piece, "row", axis=1, tiled=True)


def per_device(trial_panel, tile_values, tile_rows, tile_cols, tile_counts):
    grid_side = lax.axis_size("row")
    piece_rows = trial_panel.shape[2]
    vectors = trial_panel.shape[3]
    tile_size = tile_values.shape[3]
    block_total = piece_rows * grid_side // tile_size
    cell_tiles = tile_values[0, 0]
    rows_index = tile_rows[0, 0]
    cols_index = tile_cols[0, 0]
    used_count = tile_counts[0, 0]
    on_diagonal = (lax.axis_index("row") == lax.axis_index("col")).astype(jnp.float32)

    def product_of(source, flipped):
        grouped = source.reshape(block_total, tile_size, vectors)
        return cell_product(
            cell_tiles, rows_index, cols_index, used_count, grouped, flipped, on_diagonal
        )

    previous = trial_panel.astype(jnp.float32)
    current = previous
    rounded = trial_panel
    for degree in range(DEGREE):
        flipped = degree % 2 == 1
        if flipped:
            gathered = lax.all_gather(rounded, "col", axis=1, tiled=True)
            partial_value = product_of(gathered, True).reshape(1, grid_side, piece_rows, vectors)
            summed = lax.psum_scatter(
                partial_value.astype(jnp.bfloat16), "row", scatter_dimension=1, tiled=True
            ).astype(jnp.float32)
        else:
            gathered = gather_grid_column(rounded)
            partial_value = product_of(gathered, False).reshape(1, grid_side, piece_rows, vectors)
            summed = lax.psum_scatter(
                partial_value.astype(jnp.bfloat16), "col", scatter_dimension=1, tiled=True
            ).astype(jnp.float32)
        if degree == 0:
            updated = summed / filter_radius
        else:
            updated = 2.0 / filter_radius * summed - previous
        previous, current = (current, updated)
        rounded = updated.astype(jnp.bfloat16)
    return current


def solution(mesh):
    return jax.shard_map(
        per_device,
        mesh=mesh,
        in_specs=(
            P(("groups", "col"), "row", None, None),
            P(("groups", "row"), "col", None, None, None),
            P(("groups", "row"), "col", None),
            P(("groups", "row"), "col", None),
            P(("groups", "row"), "col"),
        ),
        out_specs=P(("groups", "row"), "col", None, None),
        check_vma=False,
    )
```

profile of v0, /device:TPU:0, one launch (start us, length us, event | category | flops | bytes accessed | tf_op | source)
XLA Modules:
  0.0 274.8 jit_solution(9338091524277522201)
XLA Ops:
  6.5 0.0 all-gather.4.cloned.1.call-start
  6.5 0.7 all-gather.4.cloned.1.call-update
  7.3 0.0 reduce-scatter.4.cloned.1.call-start
  8.0 0.7 compare_select_fusion
  8.6 0.7 compare_and_fusion
  9.3 19.1 %all-gather.4.cloned.1.call-done = bf16[1,4,512,256]{3,2,0,1:T(8,128)(2,1)} async-done(((bf16[1,1,512,256]{3,2,0,1:T(8,128)(2,1)}), bf16[1,4,512,256]{3,2,0,1:T(8,128)(2,1)}) %all-gather.4.cloned.1.call-update) | async-done | bytes 1048592 | tf_op jit(solution)/shard_map/all_gather | solution.py:32
  28.4 7.8 %gather_fusion = bf16[128,128,256]{2,1,0:T(8,128)(2,1)} fusion(bf16[16,128,256]{2,1,0:T(8,128)(2,1)} %bitcast.44, s32[1024]{0:T(1024)S(1)} %pad_clamp_fusion.1), kind=kCustom, calls=%fused_computation.clone | custom fusion | bytes 16777728 | tf_op jit(solution)/shard_map/jit(_take)/gather | solution.py:19
  36.1 11.9 %convert_bitcast_fusion.2 = bf16[128,128,256]{1,2,0:T(8,128)(2,1)} fusion(bf16[128,128,256]{2,1,0:T(8,128)(2,1)} %gather_fusion, pred[128]{0:T(512)(128)(4,1)S(1)} %compare_and_fusion, bf16[1,1,128,128,128]{4,3,2,1,0:T(8,128)(2,1)} %param.8), kind=kOutput, calls=%fused_computation.11 | convolution fusion | flops 1082130432 | bytes 20971648 | tf_op jit(solution)/shard_map/sab,sbw->saw/dot_general | solution.py:20
  48.1 0.0 copy-start
  48.1 0.0 copy-start.5
  48.1 12.5 %copy.14 = bf16[128,128,256]{2,0,1:T(8,128)(2,1)} copy(bf16[128,128,256]{1,2,0:T(8,128)(2,1)} %convert_bitcast_fusion.2) | data formatting | bytes 16777216 | tf_op jit(solution)/shard_map/convert_element_type | solution.py:22
  60.5 0.0 copy-done
  60.5 0.0 copy-done.5
  60.5 4.6 %subtract_convert_fusion.2 = bf16[16,128,256]{2,0,1:T(8,128)(2,1)S(1)} fusion(bf16[128,128,256]{2,0,1:T(8,128)(2,1)} %copy.14, bf16[16,128,256]{2,1,0:T(8,128)(2,1)S(1)} %bitcast.45, f32[]{:T(128)S(6)} %mul.25, s32[128]{0:T(128)S(1)} %bitcast.54, pred[128]{0:T(512)(128)(4,1)S(1)} %iota_compare_fusion.2), kind=kOutput, calls=%fused_computation.23 | convolution fusion | flops 136318976 | bytes 10486404 | tf_op jit(solution)/shard_map/gs,saw->gaw/dot_general | solution.py:27
  65.1 1.3 copy.16
  66.5 0.0 reduce-scatter.4.cloned.1.call-update
  66.5 0.0 all-gather.6.cloned.1.call-start
  66.5 27.3 %reduce-scatter.4.cloned.1.call-done = bf16[1,1,512,256]{3,2,1,0:T(8,128)(2,1)} async-done(((bf16[1,4,512,256]{3,2,1,0:T(8,128)(2,1)}), bf16[1,1,512,256]{3,2,1,0:T(8,128)(2,1)}) %reduce-scatter.4.cloned.1.call-update) | async-done | bytes 262160 | tf_op jit(solution)/shard_map/reduce_scatter | solution.py:67
  93.8 1.7 fusion.22
  95.5 0.0 all-gather.6.cloned.1.call-update
  95.5 0.0 reduce-scatter.6.cloned.1.call-start
  95.6 26.7 %all-gather.6.cloned.1.call-done = bf16[1,4,512,256]{3,2,0,1:T(8,128)(2,1)} async-done(((bf16[1,1,512,256]{3,2,0,1:T(8,128)(2,1)}), bf16[1,4,512,256]{3,2,0,1:T(8,128)(2,1)}) %all-gather.6.cloned.1.call-update) | async-done | bytes 1048592 | tf_op jit(solution)/shard_map/all_gather | solution.py:59
  122.3 7.8 %gather_fusion.1 = bf16[128,128,256]{2,1,0:T(8,128)(2,1)} fusion(bf16[16,128,256]{2,1,0:T(8,128)(2,1)} %bitcast.46, s32[1024]{0:T(1024)S(1)} %pad_clamp_fusion), kind=kCustom, calls=%fused_computation.1.clone | custom fusion | bytes 16777728 | tf_op jit(solution)/shard_map/jit(_take)/gather | solution.py:19
  130.1 8.9 %convert_bitcast_fusion.1 = bf16[128,128,256]{1,2,0:T(8,128)(2,1)} fusion(bf16[128,128,256]{2,1,0:T(8,128)(2,1)} %gather_fusion.1, pred[128]{0:T(512)(128)(4,1)S(1)} %compare_and_fusion.1, bf16[1,1,128,128,128]{4,3,2,1,0:T(8,128)(2,1)} %param.8), kind=kOutput, calls=%fused_computation.10 | convolution fusion | flops 1082130432 | bytes 20971648 | tf_op jit(solution)/shard_map/sba,sbw->saw/dot_general | solution.py:20
  139.0 0.0 copy-start.1
  139.0 12.5 %copy.19 = bf16[128,128,256]{2,0,1:T(8,128)(2,1)} copy(bf16[128,128,256]{1,2,0:T(8,128)(2,1)} %convert_bitcast_fusion.1) | data formatting | bytes 16777216 | tf_op jit(solution)/shard_map/convert_element_type | solution.py:22
  151.4 0.0 copy-done.1
  151.4 0.0 copy-done.6
  151.4 4.6 %subtract_convert_fusion.1 = bf16[16,128,256]{2,0,1:T(8,128)(2,1)S(1)} fusion(bf16[128,128,256]{2,0,1:T(8,128)(2,1)} %copy.19, bf16[16,128,256]{2,1,0:T(8,128)(2,1)S(1)} %bitcast.47, f32[]{:T(128)S(6)} %mul.25, s32[128]{0:T(128)S(1)} %bitcast.56, pred[128]{0:T(512)(128)(4,1)S(1)} %iota_compare_fusion.2), kind=kOutput, calls=%fused_computation.22 | convolution fusion | flops 136318976 | bytes 10486404 | tf_op jit(solution)/shard_map/gs,saw->gaw/dot_general | solution.py:27
  156.1 1.3 copy.21
  157.4 0.0 reduce-scatter.6.cloned.1.call-update
  157.4 0.2 all-gather.8.cloned.1.call-start
  157.7 24.3 %reduce-scatter.6.cloned.1.call-done = bf16[1,1,512,256]{3,2,1,0:T(8,128)(2,1)} async-done(((bf16[1,4,512,256]{3,2,1,0:T(8,128)(2,1)}), bf16[1,1,512,256]{3,2,1,0:T(8,128)(2,1)}) %reduce-scatter.6.cloned.1.call-update) | async-done | bytes 262160 | tf_op jit(solution)/shard_map/reduce_scatter | solution.py:61
  182.0 0.0 copy-done.3
  182.0 1.7 fusion.23
  183.7 0.0 all-gather.8.cloned.1.call-update
  183.8 0.0 reduce-scatter.8.cloned.1.call-start
  183.8 16.9 %all-gather.8.cloned.1.call-done = bf16[1,4,512,256]{3,2,0,1:T(8,128)(2,1)} async-done(((bf16[1,1,512,256]{3,2,0,1:T(8,128)(2,1)}), bf16[1,4,512,256]{3,2,0,1:T(8,128)(2,1)}) %all-gather.8.cloned.1.call-update) | async-done | bytes 1048592 | tf_op jit(solution)/shard_map/all_gather | solution.py:32
  200.7 7.8 %gather_fusion.2 = bf16[128,128,256]{2,1,0:T(8,128)(2,1)} fusion(bf16[16,128,256]{2,1,0:T(8,128)(2,1)} %bitcast.48, s32[1024]{0:T(1024)S(1)} %pad_clamp_fusion.1), kind=kCustom, calls=%fused_computation.2.clone | custom fusion | bytes 16777728 | tf_op jit(solution)/shard_map/jit(_take)/gather | solution.py:19
  208.4 11.9 %convert_bitcast_fusion = bf16[128,128,256]{1,2,0:T(8,128)(2,1)} fusion(bf16[128,128,256]{2,1,0:T(8,128)(2,1)} %gather_fusion.2, pred[128]{0:T(512)(128)(4,1)S(1)} %compare_and_fusion, bf16[1,1,128,128,128]{4,3,2,1,0:T(8,128)(2,1)} %param.8), kind=kOutput, calls=%fused_computation.9 | convolution fusion | flops 1082130432 | bytes 20971648 | tf_op jit(solution)/shard_map/sab,sbw->saw/dot_general | solution.py:20
  220.3 12.5 %copy.24 = bf16[128,128,256]{2,0,1:T(8,128)(2,1)} copy(bf16[128,128,256]{1,2,0:T(8,128)(2,1)} %convert_bitcast_fusion) | data formatting | bytes 16777216 | tf_op jit(solution)/shard_map/convert_element_type | solution.py:22
  232.8 0.0 copy-done.2
  232.8 4.6 %subtract_convert_fusion = bf16[16,128,256]{2,0,1:T(8,128)(2,1)S(1)} fusion(bf16[128,128,256]{2,0,1:T(8,128)(2,1)} %copy.24, bf16[16,128,256]{2,1,0:T(8,128)(2,1)S(1)} %bitcast.49, f32[]{:T(128)S(6)} %mul.25, s32[128]{0:T(128)S(1)} %bitcast.55, pred[128]{0:T(512)(128)(4,1)S(1)} %iota_compare_fusion.2), kind=kOutput, calls=%fused_computation.21 | convolution fusion | flops 136318976 | bytes 10486404 | tf_op jit(solution)/shard_map/gs,saw->gaw/dot_general | solution.py:27
  237.4 1.3 copy.26
  238.8 0.0 reduce-scatter.8.cloned.1.call-update
  238.8 27.3 %reduce-scatter.8.cloned.1.call-done = bf16[1,1,512,256]{3,2,1,0:T(8,128)(2,1)} async-done(((bf16[1,4,512,256]{3,2,1,0:T(8,128)(2,1)}), bf16[1,1,512,256]{3,2,1,0:T(8,128)(2,1)}) %reduce-scatter.8.cloned.1.call-update) | async-done | bytes 262160 | tf_op jit(solution)/shard_map/reduce_scatter | solution.py:67
  266.1 0.0 copy-done.4
  266.1 1.8 multiply_subtract_fusion
  (9 shorter events, 0.0 us)
Async XLA Ops:
  6.5 21.8 %all-gather.4.cloned.1.call-start = ((), (), s32[]{:S(2)}) async-start(), calls=%async_computation.3 | async-start | bytes 1310720 | tf_op jit(solution)/shard_map/all_gather | solution.py:32
  7.3 86.6 %reduce-scatter.4.cloned.1.call-start = ((), (), s32[]{:S(2)}) async-start(), calls=%async_computation.4 | async-start | bytes 1310720 | tf_op jit(solution)/shard_map/reduce_scatter | solution.py:67
  48.1 12.5 %copy-start = (bf16[1,4,512,256]{3,2,0,1:T(8,128)(2,1)S(1)}, bf16[1,4,512,256]{3,2,0,1:T(8,128)(2,1)}, u32[]{:S(2)}) copy-start(bf16[1,4,512,256]{3,2,0,1:T(8,128)(2,1)} %all-gather.4.cloned.1.call-done) | copy-start | bytes 3145732
  48.1 12.5 %copy-start.5 = (s32[1,1,128]{2,1,0:T(1,128)S(1)}, s32[1,1,128]{2,1,0:T(1,128)}, u32[]{:S(2)}) copy-start(s32[1,1,128]{2,1,0:T(1,128)} %param.9) | copy-start | bytes 1540
  66.5 55.8 %all-gather.6.cloned.1.call-start = ((), (), s32[]{:S(2)}) async-start(), calls=%async_computation.5 | async-start | bytes 1310720 | tf_op jit(solution)/shard_map/all_gather | solution.py:59
  95.5 86.5 %reduce-scatter.6.cloned.1.call-start = ((), (), s32[]{:S(2)}) async-start(), calls=%async_computation.6 | async-start | bytes 1310720 | tf_op jit(solution)/shard_map/reduce_scatter | solution.py:61
  139.0 12.5 %copy-start.1 = (bf16[1,4,512,256]{3,2,0,1:T(8,128)(2,1)S(1)}, bf16[1,4,512,256]{3,2,0,1:T(8,128)(2,1)}, u32[]{:S(2)}) copy-start(bf16[1,4,512,256]{3,2,0,1:T(8,128)(2,1)} %all-gather.6.cloned.1.call-done) | copy-start | bytes 3145732
  139.0 12.5 %copy-start.6 = (s32[1,1,128]{2,1,0:T(1,128)S(1)}, s32[1,1,128]{2,1,0:T(1,128)}, u32[]{:S(2)}) copy-start(s32[1,1,128]{2,1,0:T(1,128)} %param.10) | copy-start | bytes 1540
  151.4 30.6 %copy-start.3 = (bf16[1,1,512,256]{3,2,1,0:T(8,128)(2,1)S(1)}, bf16[1,1,512,256]{3,2,1,0:T(8,128)(2,1)}, u32[]{:S(2)}) copy-start(bf16[1,1,512,256]{3,2,1,0:T(8,128)(2,1)} %param.7) | copy-start | bytes 786436
  157.4 43.2 %all-gather.8.cloned.1.call-start = ((), (), s32[]{:S(2)}) async-start(), calls=%async_computation.7 | async-start | bytes 1310720 | tf_op jit(solution)/shard_map/all_gather | solution.py:32
  183.8 82.4 %reduce-scatter.8.cloned.1.call-start = ((), (), s32[]{:S(2)}) async-start(), calls=%async_computation.8 | async-start | bytes 1310720 | tf_op jit(solution)/shard_map/reduce_scatter | solution.py:67
  220.3 12.5 %copy-start.2 = (bf16[1,4,512,256]{3,2,0,1:T(8,128)(2,1)S(1)}, bf16[1,4,512,256]{3,2,0,1:T(8,128)(2,1)}, u32[]{:S(2)}) copy-start(bf16[1,4,512,256]{3,2,0,1:T(8,128)(2,1)} %all-gather.8.cloned.1.call-done) | copy-start | bytes 3145732
  232.8 33.3 %copy-start.4 = (bf16[1,1,512,256]{3,2,1,0:T(8,128)(2,1)S(1)}, bf16[1,1,512,256]{3,2,1,0:T(8,128)(2,1)}, u32[]{:S(2)}) copy-start(bf16[1,1,512,256]{3,2,1,0:T(8,128)(2,1)} %reduce-scatter.4.cloned.1.call-done) | copy-start | bytes 786436
Sparse Core Ops, SparseCore 0:
  8.9 19.4 all-gather.3
  66.6 27.1 reduce-scatter.3
  95.7 26.5 all-gather.5
  157.6 24.3 reduce-scatter.5
  183.9 16.7 all-gather.7
  238.9 27.1 reduce-scatter.7
where the time goes:
time: 276 us; the launch traced here: 275 us
  waiting for transfers between devices  142 us (51%)
  local copies, waits for them, and re-layouts  64.8 us (23%)
  matrix products  46.6 us (17%)
  between operations  14.2 us (5%)
  other arithmetic  6.62 us (2%)
    reduce_scatter x2, waiting for transfers between devices, per_device(): lax.psum_scatter(partial_value.astype(jnp.bfloat16), 'col', scatter_dimen...  54.6 us
    convert_element_type x3, local copies, waits for them, and re-layouts, cell_product(): products = jnp.einsum(einsum_form, cell_tiles, picked, preferred_element_...  37.4 us
    all_gather x2, waiting for transfers between devices, gather_grid_column(): return lax.all_gather(piece, 'row', axis=1, tiled=True)  35.9 us
    dot_general x3, matrix products, cell_product(): jnp.einsum(einsum_form, cell_tiles, picked, preferred_element_type=jnp.fl...  32.7 us
    all_gather x1, waiting for transfers between devices, per_device(): gathered = lax.all_gather(rounded, 'col', axis=1, tiled=True)  26.7 us
    reduce_scatter x1, waiting for transfers between devices, per_device(): lax.psum_scatter(partial_value.astype(jnp.bfloat16), 'row', scatter_dimen...  24.3 us
    gather x3, local copies, waits for them, and re-layouts, cell_product(): picked = jnp.take(source, pick_index, axis=0)  23.3 us
    dot_general x3, matrix products, cell_product(): jnp.einsum('gs,saw->gaw', placing, products, preferred_element_type=jnp.f...  13.8 us
  transfers between devices with their start and end apart: 6, of which 6 were waited for; matrix products, arithmetic and copies ran while one was open for 0% of the time, Pallas kernels for 0%

commit v1 on v0

v1 whole, which is shorter than its diff:
```python
import functools

import jax
import jax.numpy as jnp
from jax import lax
from jax.experimental import pallas as pl
from jax.experimental.pallas import tpu as pltpu
from jax.sharding import PartitionSpec as P

MESH = pl.DeviceIdType.MESH
LANES = 128
filter_center = 0.5
filter_radius = 1.5
F32 = jnp.float32
BF16 = jnp.bfloat16


class Line:
    def __init__(self, size, place, peer):
        self.size, self.place, self.peer = size, place, peer

    def copy(self, buf, side, piece, send, recv, slot=None):
        target = self.peer(1 if side == 0 else -1)
        ref = buf.at[piece] if slot is None else buf.at[side, piece]
        return pltpu.make_async_remote_copy(
            src_ref=ref, dst_ref=ref, send_sem=send.at[side, piece], recv_sem=recv.at[side, piece],
            device_id=target, device_id_type=MESH)

    def arrival(self, buf, side, piece, send, recv, slot=None):
        self.copy(buf, side, piece, send, recv, slot).wait_recv()

    def sum_moves(self, t):
        n, i = self.size, self.place
        j = n - 1 - i
        return ((0, (t >= i) & (t <= n - 2), n - 1 - t + i, i > 0),
                (1, (t >= j) & (t <= n - 2), t - j, i < n - 1))

    def sum_step(self, t, buf, part, send, recv):
        for side, active, piece, inner in self.sum_moves(t):
            @pl.when(active)
            def _():
                @pl.when(inner)
                def _():
                    self.arrival(buf, side, piece, send, recv, 1)
                    buf[side, piece] = (part[piece] + buf[side, piece].astype(F32)).astype(BF16)

                @pl.when(jnp.logical_not(inner))
                def _():
                    buf[side, piece] = part[piece].astype(BF16)

                self.copy(buf, side, piece, send, recv, 1).start()

    def sum_finish(self, buf, part, send, recv, total):
        i = self.place
        total[...] = part[i]
        for side, inner in ((0, i > 0), (1, i < self.size - 1)):
            @pl.when(inner)
            def _():
                self.arrival(buf, side, i, send, recv, 1)
                total[...] += buf[side, i].astype(F32)

    def sum_drain(self, buf, send, recv):
        for t in range(self.size - 1):
            for side, active, piece, _ in self.sum_moves(t):
                @pl.when(active)
                def _():
                    self.copy(buf, side, piece, send, recv, 1).wait_send()

    def spread_moves(self, s):
        n, i = self.size, self.place
        return ((0, i - s >= 0, i - s, i < n - 1), (1, i + s <= n - 1, i + s, i > 0))

    def spread_step(self, s, buf, send, recv, arrived=None):
        for side, present, piece, onward in self.spread_moves(s):
            @pl.when(present)
            def _():
                if s > 0:
                    self.arrival(buf, side, piece, send, recv)

                @pl.when(onward)
                def _():
                    self.copy(buf, side, piece, send, recv).start()

                if s > 0 and arrived is not None:
                    arrived(piece)

    def spread_drain(self, buf, send, recv):
        for s in range(self.size):
            for side, present, piece, onward in self.spread_moves(s):
                @pl.when(present & onward)
                def _():
                    self.copy(buf, side, piece, send, recv).wait_send()


def kernel(sizes, slot_ref, trial_ref, tiles_hbm, out_ref,
           tiles, dense, flipped, xg, yg1, yg2, part0, part1, part2, acc, y1, zsum0, zsum2, xsum, pair_out, pair_in,
           tile_sem, xg_send, xg_recv, xp_send, xp_recv, zs0_send, zs0_recv, zg_send, zg_recv,
           pr_send, pr_recv, xs_send, xs_recv, yg_send, yg_recv, yp_send, yp_recv, zs2_send, zs2_recv):
    row_size, col_size, blocks, tile, slots, streams = sizes
    x_size = row_size // 2
    piece_rows = trial_ref.shape[2]
    row, col = lax.axis_index("row"), lax.axis_index("col")
    x, core = lax.div(row, 2), lax.rem(row, 2)
    sibling = {"row": row + 1 - 2 * core}
    zline = Line(col_size, col, lambda d: {"col": col + d})
    xline = Line(x_size, x, lambda d: {"row": row + 2 * d})
    shift = jnp.where(row == col, filter_center, 0.0).astype(F32)

    tile_copy = pltpu.make_async_copy(tiles_hbm.at[0, 0], tiles.at[pl.ds(0, slots)], tile_sem)
    tile_copy.start()

    barrier = pltpu.get_barrier_semaphore()
    pl.semaphore_signal(barrier, inc=1, device_id=sibling, device_id_type=MESH)
    for line in (zline, xline):
        for d, there in ((-1, line.place > 0), (1, line.place < line.size - 1)):
            @pl.when(there)
            def _():
                pl.semaphore_signal(barrier, inc=1, device_id=line.peer(d), device_id_type=MESH)
    peers = 1
    for line in (zline, xline):
        peers += (line.place > 0).astype(jnp.int32) + (line.place < line.size - 1).astype(jnp.int32)
    pl.semaphore_wait(barrier, peers)

    def pair_copy(src, dst, send, recv):
        return pltpu.make_async_remote_copy(
            src_ref=src, dst_ref=dst, send_sem=send, recv_sem=recv, device_id=sibling, device_id_type=MESH)

    def gather_row(buf, s, send, recv, psend, precv):
        mine = Rows(buf, s, core)

        def to_sibling(place):
            ref = buf.at[s, 2 * place + core]
            pair_copy(ref, ref, psend.at[s, place], precv.at[s, place]).start()

        for step in range(x_size):
            xline.spread_step(step, mine, send.at[s], recv.at[s], to_sibling)
            if step == 0:
                to_sibling(x)
            yield
        for place in range(x_size):
            ref = buf.at[s, 2 * place + 1 - core]
            pair_copy(ref, ref, psend.at[s, place], precv.at[s, place]).wait_recv()

    def gather_row_drain(buf, s, send, recv, psend, precv):
        xline.spread_drain(Rows(buf, s, core), send.at[s], recv.at[s])
        for place in range(x_size):
            ref = buf.at[s, 2 * place + core]
            pair_copy(ref, ref, psend.at[s, place], precv.at[s, place]).wait_send()

    def product(matrix, source, piece, s, target):
        count = min(piece_rows, 256)

        @pl.loop(0, piece_rows // count)
        def _(k):
            inside = pl.ds(pl.multiple_of(k * count, count), count)
            rows = pl.ds(pl.multiple_of(piece * piece_rows + k * count, count), count)
            panel = source[s].reshape(row_size * piece_rows, LANES)
            value = jnp.dot(matrix[rows, :], panel, preferred_element_type=F32)
            target[inside, :] = (value - shift * source[s, piece, inside, :].astype(F32)).astype(target.dtype)

    def build(matrix, turned):
        per = blocks // 4
        for quarter in range(4):
            @pl.loop(quarter * per * blocks // 4, (quarter + 1) * per * blocks // 4)
            def _(group):
                for inner in range(4):
                    place = group * 4 + inner
                    i, j = lax.div(place, blocks), lax.rem(place, blocks)
                    if turned:
                        value = tiles[slot_ref[j * blocks + i]].T
                    else:
                        value = tiles[slot_ref[place]]
                    rows = pl.ds(pl.multiple_of(i * tile, tile), tile)
                    lanes = pl.ds(pl.multiple_of(j * tile, tile), tile)
                    matrix[rows, lanes] = value
            yield

        @pl.loop(0, blocks)
        def _(i):
            at = pl.ds(pl.multiple_of(i * tile, tile), tile)
            value = tiles[slot_ref[blocks * blocks + i]]
            matrix[at, at] += value.T if turned else value
        yield

    def products_and_sums(s, matrix, source, part, buf, send, recv):
        for t in range(col_size):
            piece = jnp.where(t < col, t, col_size - 1 - t + col)
            product(matrix, source, piece, s, part.at[s, piece])
            if t < col_size - 1:
                zline.sum_step(t, buf.at[s], part.at[s], send.at[s], recv.at[s])
                yield

    def stream(s):
        lanes = slice(s * LANES, (s + 1) * LANES)
        xg[s, row] = trial_ref[0, 0, :, lanes]
        yield from gather_row(xg, s, xg_send, xg_recv, xp_send, xp_recv)
        yield
        yield from products_and_sums(s, dense, xg, part0, zsum0, zs0_send, zs0_recv)
        zline.sum_finish(zsum0.at[s], part0.at[s], zs0_send.at[s], zs0_recv.at[s], acc)
        value = acc[...] / filter_radius
        y1[s] = value
        yg1[s, col] = value.astype(BF16)
        for step in range(col_size):
            zline.spread_step(step, yg1.at[s], zg_send.at[s], zg_recv.at[s])
            yield
        for place in range(x_size):
            product(flipped, yg1, 2 * place + 1 - core, s, pair_out.at[s, place])
        pair = pair_copy(pair_out.at[s], pair_in.at[s], pr_send.at[s], pr_recv.at[s])
        pair.start()
        for place in range(x_size):
            product(flipped, yg1, 2 * place + core, s, part1.at[s, place])
        yield
        pair.wait_recv()
        part1[s] += pair_in[s].astype(F32)
        for t in range(x_size - 1):
            xline.sum_step(t, xsum.at[s], part1.at[s], xs_send.at[s], xs_recv.at[s])
            yield
        xline.sum_finish(xsum.at[s], part1.at[s], xs_send.at[s], xs_recv.at[s], acc)
        value = (2.0 / filter_radius) * acc[...] - trial_ref[0, 0, :, lanes].astype(F32)
        yg2[s, row] = value.astype(BF16)
        yield from gather_row(yg2, s, yg_send, yg_recv, yp_send, yp_recv)
        yield
        yield from products_and_sums(s, dense, yg2, part2, zsum2, zs2_send, zs2_recv)
        zline.sum_finish(zsum2.at[s], part2.at[s], zs2_send.at[s], zs2_recv.at[s], acc)
        out_ref[0, 0, :, lanes] = (2.0 / filter_radius) * acc[...] - y1[s]

    def stream_drain(s):
        gather_row_drain(xg, s, xg_send, xg_recv, xp_send, xp_recv)
        zline.sum_drain(zsum0.at[s], zs0_send.at[s], zs0_recv.at[s])
        zline.spread_drain(yg1.at[s], zg_send.at[s], zg_recv.at[s])
        pair_copy(pair_out.at[s], pair_in.at[s], pr_send.at[s], pr_recv.at[s]).wait_send()
        xline.sum_drain(xsum.at[s], xs_send.at[s], xs_recv.at[s])
        gather_row_drain(yg2, s, yg_send, yg_recv, yp_send, yp_recv)
        zline.sum_drain(zsum2.at[s], zs2_send.at[s], zs2_recv.at[s])

    programs = [stream(s) for s in range(streams)]

    def advance(which, count=1):
        for _ in range(count):
            next(which, None)

    first = programs[0]
    advance(first)
    for other in programs[1:]:
        advance(other)
    tiles[slots] = jnp.zeros((tile, tile), BF16)
    tile_copy.wait()
    for _ in build(dense, False):
        pass
    turned = build(flipped, True)
    gathers = x_size
    advance(first, gathers)
    sums = col_size - 1
    advance(first)
    for other in programs[1:]:
        advance(other, gathers)
    advance(turned)
    for _ in range(sums - 1):
        advance(first)
        advance(turned)
    advance(first)
    for _ in turned:
        pass
    for _ in range(col_size - 1):
        for other in programs[1:]:
            advance(other)
        advance(first)
    advance(first)
    live = [True] * streams
    while any(live):
        for s in list(range(1, streams)) + [0]:
            if live[s]:
                try:
                    next(programs[s])
                except StopIteration:
                    live[s] = False
    for s in range(streams):
        stream_drain(s)


class Rows:
    def __init__(self, buf, s, core):
        self.buf, self.s, self.core = buf, s, core

    @property
    def at(self):
        return self

    def __getitem__(self, place):
        return self.buf.at[self.s, 2 * place + self.core]


def slot_table(rows, cols, count, blocks, slots):
    order = lax.iota(jnp.int32, slots)
    place = jnp.where(order < count, rows * blocks + cols, -1)
    hit = place[None, :] == lax.iota(jnp.int32, blocks * blocks)[:, None]
    first = jnp.min(jnp.where(hit, order[None, :], slots), axis=1)
    diagonal = lax.iota(jnp.int32, blocks) * (blocks + 1)
    hit = place[None, :] == diagonal[:, None]
    low = jnp.min(jnp.where(hit, order[None, :], slots), axis=1)
    high = jnp.max(jnp.where(hit, order[None, :], -1), axis=1)
    second = jnp.where(high > low, high, slots)
    return jnp.concatenate([first, second])


def per_device(trial_panel, tile_values, tile_rows, tile_cols, tile_counts):
    row_size, col_size = lax.axis_size("row"), lax.axis_size("col")
    piece_rows, vectors = trial_panel.shape[2:]
    slots, tile = tile_values.shape[2:4]
    blocks = piece_rows * row_size // tile
    order = piece_rows * row_size
    streams = vectors // LANES
    x_size = row_size // 2
    table = slot_table(tile_rows[0, 0], tile_cols[0, 0], tile_counts[0, 0], blocks, slots)
    piece = (piece_rows, LANES)

    def vmem(shape, dtype=BF16):
        return pltpu.VMEM(shape, dtype)

    def sems(*shape):
        return [pltpu.SemaphoreType.DMA(shape)] * 2

    scratch = [
        vmem((slots + 1, tile, tile)), vmem((order, order)), vmem((order, order)),
        vmem((streams, row_size) + piece), vmem((streams, col_size) + piece), vmem((streams, row_size) + piece),
        vmem((streams, col_size) + piece, F32), vmem((streams, x_size) + piece, F32),
        vmem((streams, col_size) + piece, F32), vmem(piece, F32), vmem((streams,) + piece, F32),
        vmem((streams, 2, col_size) + piece), vmem((streams, 2, col_size) + piece),
        vmem((streams, 2, x_size) + piece),
        vmem((streams, x_size) + piece), vmem((streams, x_size) + piece),
        pltpu.SemaphoreType.DMA,
        *sems(streams, 2, x_size), *sems(streams, x_size),
        *sems(streams, 2, col_size), *sems(streams, 2, col_size),
        *sems(streams), *sems(streams, 2, x_size),
        *sems(streams, 2, x_size), *sems(streams, x_size),
        *sems(streams, 2, col_size),
    ]
    sizes = (row_size, col_size, blocks, tile, slots, streams)
    return pl.pallas_call(
        functools.partial(kernel, sizes),
        out_shape=jax.ShapeDtypeStruct((1, 1, piece_rows, vectors), F32),
        in_specs=[pl.BlockSpec(memory_space=pltpu.SMEM), pl.BlockSpec(memory_space=pltpu.VMEM),
                  pl.BlockSpec(memory_space=pl.ANY)],
        out_specs=pl.BlockSpec(memory_space=pltpu.VMEM),
        scratch_shapes=scratch,
        compiler_params=pltpu.CompilerParams(
            collective_id=0, has_side_effects=True, vmem_limit_bytes=56 * 1024 * 1024),
        cost_estimate=pl.CostEstimate(
            flops=6 * order * order * vectors, bytes_accessed=slots * tile * tile * 2, transcendentals=0),
    )(table, trial_panel, tile_values)


def solution(mesh):
    return jax.shard_map(
        per_device,
        mesh=mesh,
        in_specs=(
            P(("groups", "col"), "row", None, None),
            P(("groups", "row"), "col", None, None, None),
            P(("groups", "row"), "col", None),
            P(("groups", "row"), "col", None),
            P(("groups", "row"), "col"),
        ),
        out_specs=P(("groups", "row"), "col", None, None),
        check_vma=False,
    )
```

time: 276 us -> 94.3 us (0.34)
  waiting for transfers between devices: 142 us -> 0 us
  Pallas kernels: 0 us -> 89.9 us
  local copies, waits for them, and re-layouts: 64.8 us -> 1.87 us
  matrix products: 46.6 us -> 0 us
  between operations: 14.2 us -> 0.67 us
  other arithmetic: 6.62 us -> 1.57 us
    pallas_call x0 -> x1, Pallas kernels: none -> 89.9 us  [per_device(): pl.pallas_call(functools.partial(kernel, sizes), out_shape=jax.ShapeDtype...]
    reduce_scatter x3 -> x0, waiting for transfers between devices: 78.9 us -> none  [the longest x2 54.6 us: per_device(): lax.psum_scatter(partial_value.astype(jnp.bfloat16), 'col', scatter_dimen...]
    all_gather x3 -> x0, waiting for transfers between devices: 62.6 us -> none  [the longest x2 35.9 us: gather_grid_column(): return lax.all_gather(piece, 'row', axis=1, tiled=True)]
    dot_general x6 -> x0, matrix products: 46.6 us -> none  [the longest x3 32.7 us: cell_product(): jnp.einsum(einsum_form, cell_tiles, picked, preferred_element_type=jnp.fl...]
    convert_element_type x6 -> x0, local copies, waits for them, and re-layouts: 41.4 us -> none  [the longest x3 37.4 us: cell_product(): products = jnp.einsum(einsum_form, cell_tiles, picked, preferred_element_...]
    gather x3 -> x0, local copies, waits for them, and re-layouts: 23.3 us -> none  [cell_product(): picked = jnp.take(source, pick_index, axis=0)]
    convert_element_type x2 -> x0, other arithmetic: 3.43 us -> none  [per_device(): rounded = updated.astype(jnp.bfloat16)]
  transfers between devices with their start and end apart: 6 -> 0, of which waited for: 6 -> 0; matrix products, arithmetic and copies ran while one was open for 0% -> 0% of each run, Pallas kernels for 0% -> 0%
where the time goes in v1:
time: 94.3 us; the launch traced here: 94.1 us
  Pallas kernels  89.9 us (95%)
  local copies, waits for them, and re-layouts  1.87 us (2%)
  other arithmetic  1.57 us (2%)
    pallas_call x1, Pallas kernels, per_device(): pl.pallas_call(functools.partial(kernel, sizes), out_shape=jax.ShapeDtype...  89.9 us

profile of v1, /device:TPU:0, one launch (start us, length us, event | category | flops | bytes accessed | tf_op | source)
XLA Modules:
  0.0 94.1 jit_solution(2571142392531867948)
XLA Ops:
  0.7 0.7 compare_select_fusion.3
  1.3 0.2 fusion.1
  1.5 0.1 select_reduce_fusion
  1.6 0.6 pad_add_fusion.slot_ref
  2.2 89.9 %shard_map.55 = f32[1,1,512,256]{3,2,1,0:T(8,128)} custom-call(s32[272]{0:T(512)} %pad_add_fusion.slot_ref, bf16[1,1,512,256]{3,2,1,0:T(8,128)(2,1)} %trial_ref.1, bf16[1,1,128,128,128]{4,3,2,1,0:T(8,128)(2,1)} %tiles_hbm.1), custom_call_target="tpu_custom_call" | custom-call | flops 6442450944 | bytes 4194304 | tf_op jit(solution)/shard_map/pallas_call | solution.py:339
  92.2 1.9 %copy.8 = f32[1,1,512,256]{3,2,1,0:T(8,128)} copy(f32[1,1,512,256]{3,2,1,0:T(8,128)} %shard_map.55) | data formatting | bytes 1048576
  (2 shorter events, 0.0 us)

commit v2 on v1

v2 whole, which is shorter than its diff:
```python
import functools

import jax
import jax.numpy as jnp
from jax import lax
from jax.experimental import pallas as pl
from jax.experimental.pallas import tpu as pltpu
from jax.sharding import PartitionSpec as P

MESH = pl.DeviceIdType.MESH
LANES = 128
filter_center = 0.5
filter_radius = 1.5
F32 = jnp.float32
BF16 = jnp.bfloat16


class Peers:
    def __init__(self, size, place, device):
        self.size, self.place, self.device = size, place, device

    def others(self):
        for d in range(1, self.size):
            yield lax.rem(self.place + d, self.size)

    def copy(self, src, dst, to, send, recv):
        return pltpu.make_async_remote_copy(
            src_ref=src, dst_ref=dst, send_sem=send, recv_sem=recv,
            device_id=self.device(to), device_id_type=MESH)

    def spread(self, buf, send, recv):
        here = buf(self.place)
        for peer in self.others():
            self.copy(here, here, peer, send.at[peer], recv.at[self.place]).start()

    def spread_wait(self, buf, send, recv, peer):
        self.copy(buf(peer), buf(peer), peer, send.at[peer], recv.at[peer]).wait_recv()

    def spread_drain(self, buf, send, recv):
        for peer in self.others():
            self.copy(buf(peer), buf(peer), peer, send.at[peer], recv.at[peer]).wait_send()

    def give(self, outgoing, incoming, to, send, recv):
        self.copy(outgoing.at[to], incoming.at[self.place], to, send.at[to], recv.at[self.place]).start()

    def collect(self, outgoing, incoming, own, send, recv):
        total = own
        for peer in self.others():
            self.copy(outgoing.at[peer], incoming.at[peer], peer, send.at[peer], recv.at[peer]).wait_recv()
            total = total + incoming[peer].astype(F32)
        return total

    def give_drain(self, outgoing, incoming, send, recv):
        for peer in self.others():
            self.copy(outgoing.at[peer], incoming.at[peer], peer, send.at[peer], recv.at[peer]).wait_send()


def kernel(sizes, slot_ref, trial_ref, tiles_hbm, out_ref,
           tiles, dense, flipped, xg, yg1, yg2, own, part1, y1, zout0, zin0, zout2, zin2, zrel0, zrel2, xout, xin, pair_out, pair_in,
           tile_sem, xg_send, xg_recv, xp_send, xp_recv, zs0_send, zs0_recv, zg_send, zg_recv,
           pr_send, pr_recv, xs_send, xs_recv, yg_send, yg_recv, yp_send, yp_recv, zs2_send, zs2_recv,
           zr0_recv, zr2_recv, zf_send):
    row_size, col_size, blocks, tile, slots, streams = sizes
    x_size = row_size // 2
    piece_rows = trial_ref.shape[2]
    row, col = lax.axis_index("row"), lax.axis_index("col")
    x, core = lax.div(row, 2), lax.rem(row, 2)
    sibling = {"row": row + 1 - 2 * core}
    zline = Peers(col_size, col, lambda i: {"col": i})
    xline = Peers(x_size, x, lambda i: {"row": 2 * i + core})
    shift = jnp.where(row == col, filter_center, 0.0).astype(F32)

    tile_copy = pltpu.make_async_copy(tiles_hbm.at[0, 0], tiles.at[pl.ds(0, slots)], tile_sem)
    tile_copy.start()

    barrier = pltpu.get_barrier_semaphore()
    pl.semaphore_signal(barrier, inc=1, device_id=sibling, device_id_type=MESH)
    for line in (zline, xline):
        for peer in line.others():
            pl.semaphore_signal(barrier, inc=1, device_id=line.device(peer), device_id_type=MESH)
    pl.semaphore_wait(barrier, col_size + x_size - 1)

    def pair_copy(src, dst, send, recv):
        return pltpu.make_async_remote_copy(
            src_ref=src, dst_ref=dst, send_sem=send, recv_sem=recv, device_id=sibling, device_id_type=MESH)

    def gather_row(buf, s, send, recv, psend, precv):
        def mine(place):
            return buf.at[s, 2 * place + core]

        def to_sibling(place):
            pair_copy(mine(place), mine(place), psend.at[s, place], precv.at[s, place]).start()

        xline.spread(mine, send.at[s], recv.at[s])
        to_sibling(x)
        yield
        for peer in xline.others():
            xline.spread_wait(mine, send.at[s], recv.at[s], peer)
            to_sibling(peer)
        yield
        for place in range(x_size):
            ref = buf.at[s, 2 * place + 1 - core]
            pair_copy(ref, ref, psend.at[s, place], precv.at[s, place]).wait_recv()

    def gather_row_drain(buf, s, send, recv, psend, precv):
        def mine(place):
            return buf.at[s, 2 * place + core]

        xline.spread_drain(mine, send.at[s], recv.at[s])
        for place in range(x_size):
            pair_copy(mine(place), mine(place), psend.at[s, place], precv.at[s, place]).wait_send()

    def product(matrix, source, piece, s, target):
        count = min(piece_rows, 256)

        @pl.loop(0, piece_rows // count)
        def _(k):
            inside = pl.ds(pl.multiple_of(k * count, count), count)
            rows = pl.ds(pl.multiple_of(piece * piece_rows + k * count, count), count)
            panel = source[s].reshape(row_size * piece_rows, LANES)
            value = jnp.dot(matrix[rows, :], panel, preferred_element_type=F32)
            target[inside, :] = (value - shift * source[s, piece, inside, :].astype(F32)).astype(target.dtype)

    def build(matrix, turned):
        per = blocks // 4
        for quarter in range(4):
            @pl.loop(quarter * per * blocks // 4, (quarter + 1) * per * blocks // 4)
            def _(group):
                for inner in range(4):
                    place = group * 4 + inner
                    i, j = lax.div(place, blocks), lax.rem(place, blocks)
                    if turned:
                        value = tiles[slot_ref[j * blocks + i]].T
                    else:
                        value = tiles[slot_ref[place]]
                    rows = pl.ds(pl.multiple_of(i * tile, tile), tile)
                    lanes = pl.ds(pl.multiple_of(j * tile, tile), tile)
                    matrix[rows, lanes] = value
            yield

        @pl.loop(0, blocks)
        def _(i):
            at = pl.ds(pl.multiple_of(i * tile, tile), tile)
            value = tiles[slot_ref[blocks * blocks + i]]
            matrix[at, at] += value.T if turned else value
        yield

    half = col_size // 2
    low = col < half
    base, gate = jnp.where(low, 0, half), jnp.where(low, half - 1, half)
    far_base, far_gate = jnp.where(low, half, 0), jnp.where(low, half, half - 1)
    at_gate = col == gate
    side = jnp.where(low, 0, 1)
    near = [lax.rem(col - base + d, half) + base for d in range(1, half)]

    def products_given(s, source, outgoing, relayed, incoming, send, recv, rsend, rrecv):
        for k in range(half):
            piece = far_base + k
            product(dense, source, piece, s, outgoing.at[s, piece])

            @pl.when(jnp.logical_not(at_gate))
            def _():
                place = col - base - side
                zline.copy(outgoing.at[s, piece], relayed.at[s, place, k], gate, send.at[s, piece],
                           rrecv.at[s, place, k]).start()
        for peer in near:
            product(dense, source, peer, s, outgoing.at[s, peer])
            zline.copy(outgoing.at[s, peer], incoming.at[s, col], peer, send.at[s, peer], recv.at[s, col]).start()
        product(dense, source, col, s, own.at[s])

    def relay_sums(s, outgoing, relayed, incoming, send, recv, rsend, rrecv):
        @pl.when(at_gate)
        def _():
            for k in range(half):
                piece = far_base + k
                total = outgoing[s, piece].astype(F32)
                for place in range(half - 1):
                    ref = relayed.at[s, place, k]
                    zline.copy(outgoing.at[s, piece], ref, far_gate, send.at[s, piece], rrecv.at[s, place, k]).wait_recv()
                    total = total + relayed[s, place, k].astype(F32)
                outgoing[s, piece] = total.astype(BF16)
                zline.copy(outgoing.at[s, piece], incoming.at[s, col], piece, send.at[s, piece], recv.at[s, col]).start()

    def collected(s, outgoing, incoming, send, recv):
        total = own[s]
        for peer in near + [far_gate]:
            zline.copy(outgoing.at[s, peer], incoming.at[s, peer], peer, send.at[s, peer], recv.at[s, peer]).wait_recv()
            total = total + incoming[s, peer].astype(F32)
        return total

    def given_drain(s, outgoing, incoming, send, recv):
        for piece in near + [far_base + k for k in range(half)]:
            zline.copy(outgoing.at[s, piece], incoming.at[s, piece], piece, send.at[s, piece], recv.at[s, piece]).wait_send()

    def spread_copy(s, piece, to, sem):
        return zline.copy(yg1.at[s, piece], yg1.at[s, piece], to, sem, zg_recv.at[s, piece])

    def spread_out(s):
        spread_copy(s, col, far_gate, zg_send.at[s, far_gate]).start()
        for peer in near:
            spread_copy(s, col, peer, zg_send.at[s, peer]).start()

    def relay_pieces(s):
        @pl.when(at_gate)
        def _():
            for k in range(half):
                piece = far_base + (k if half == 1 else jnp.where(low, k, half - 1 - k))
                spread_copy(s, piece, far_gate, zg_send.at[s, far_gate]).wait_recv()
                for place, peer in enumerate(near):
                    spread_copy(s, piece, peer, zf_send.at[s, k, place]).start()

    def spread_arrived(s):
        for peer in near:
            spread_copy(s, peer, peer, zg_send.at[s, peer]).wait_recv()

        @pl.when(jnp.logical_not(at_gate))
        def _():
            for k in range(half):
                spread_copy(s, far_base + k, gate, zg_send.at[s, far_gate]).wait_recv()

    def spread_out_drain(s):
        for peer in near + [far_gate]:
            spread_copy(s, col, peer, zg_send.at[s, peer]).wait_send()

        @pl.when(at_gate)
        def _():
            for k in range(half):
                for place, peer in enumerate(near):
                    spread_copy(s, far_base + k, peer, zf_send.at[s, k, place]).wait_send()

    def stream(s):
        lanes = slice(s * LANES, (s + 1) * LANES)
        xg[s, row] = trial_ref[0, 0, :, lanes]
        yield from gather_row(xg, s, xg_send, xg_recv, xp_send, xp_recv)
        first = (zout0, zrel0, zin0, zs0_send, zs0_recv, None, zr0_recv)
        products_given(s, xg, *first)
        yield
        relay_sums(s, *first)
        yield
        value = collected(s, zout0, zin0, zs0_send, zs0_recv) / filter_radius
        y1[s] = value
        yg1[s, col] = value.astype(BF16)
        spread_out(s)
        yield
        relay_pieces(s)
        yield
        spread_arrived(s)
        for place in range(x_size):
            product(flipped, yg1, 2 * place + 1 - core, s, pair_out.at[s, place])
        pair = pair_copy(pair_out.at[s], pair_in.at[s], pr_send.at[s], pr_recv.at[s])
        pair.start()
        for place in range(x_size):
            product(flipped, yg1, 2 * place + core, s, part1.at[s, place])
        yield
        pair.wait_recv()
        for peer in xline.others():
            xout[s, peer] = (part1[s, peer] + pair_in[s, peer].astype(F32)).astype(BF16)
            xline.give(xout.at[s], xin.at[s], peer, xs_send.at[s], xs_recv.at[s])
        yield
        value = part1[s, x] + pair_in[s, x].astype(F32)
        value = xline.collect(xout.at[s], xin.at[s], value, xs_send.at[s], xs_recv.at[s])
        value = (2.0 / filter_radius) * value - trial_ref[0, 0, :, lanes].astype(F32)
        yg2[s, row] = value.astype(BF16)
        yield from gather_row(yg2, s, yg_send, yg_recv, yp_send, yp_recv)
        last = (zout2, zrel2, zin2, zs2_send, zs2_recv, None, zr2_recv)
        products_given(s, yg2, *last)
        yield
        relay_sums(s, *last)
        yield
        value = collected(s, zout2, zin2, zs2_send, zs2_recv)
        out_ref[0, 0, :, lanes] = (2.0 / filter_radius) * value - y1[s]

    def stream_drain(s):
        gather_row_drain(xg, s, xg_send, xg_recv, xp_send, xp_recv)
        given_drain(s, zout0, zin0, zs0_send, zs0_recv)
        spread_out_drain(s)
        pair_copy(pair_out.at[s], pair_in.at[s], pr_send.at[s], pr_recv.at[s]).wait_send()
        xline.give_drain(xout.at[s], xin.at[s], xs_send.at[s], xs_recv.at[s])
        gather_row_drain(yg2, s, yg_send, yg_recv, yp_send, yp_recv)
        given_drain(s, zout2, zin2, zs2_send, zs2_recv)

    programs = [stream(s) for s in range(streams)]

    def advance(s):
        next(programs[s], None)

    for s in range(streams):
        advance(s)
    tiles[slots] = jnp.zeros((tile, tile), BF16)
    tile_copy.wait()
    for _ in build(dense, False):
        pass
    turned = build(flipped, True)
    for s in range(streams):
        advance(s)
    done, lag = [2] * streams, 1
    for turn in range(2, 13 + lag * (streams - 1)):
        for s in range(streams):
            if done[s] < 13 and turn >= 2 + lag * s:
                advance(s)
                done[s] += 1
        if turn < 5:
            next(turned, None)
        elif turn == 5:
            for _ in turned:
                pass
    for s in range(streams):
        stream_drain(s)


def slot_table(rows, cols, count, blocks, slots):
    order = lax.iota(jnp.int32, slots)
    place = jnp.where(order < count, rows * blocks + cols, -1)
    hit = place[None, :] == lax.iota(jnp.int32, blocks * blocks)[:, None]
    first = jnp.min(jnp.where(hit, order[None, :], slots), axis=1)
    diagonal = lax.iota(jnp.int32, blocks) * (blocks + 1)
    hit = place[None, :] == diagonal[:, None]
    low = jnp.min(jnp.where(hit, order[None, :], slots), axis=1)
    high = jnp.max(jnp.where(hit, order[None, :], -1), axis=1)
    second = jnp.where(high > low, high, slots)
    return jnp.concatenate([first, second])


def per_device(trial_panel, tile_values, tile_rows, tile_cols, tile_counts):
    row_size, col_size = lax.axis_size("row"), lax.axis_size("col")
    piece_rows, vectors = trial_panel.shape[2:]
    slots, tile = tile_values.shape[2:4]
    blocks = piece_rows * row_size // tile
    order = piece_rows * row_size
    streams = vectors // LANES
    x_size = row_size // 2
    table = slot_table(tile_rows[0, 0], tile_cols[0, 0], tile_counts[0, 0], blocks, slots)
    piece = (piece_rows, LANES)
    relay = (max(col_size // 2 - 1, 1), col_size // 2)

    def vmem(shape, dtype=BF16):
        return pltpu.VMEM(shape, dtype)

    def sems(*shape):
        return [pltpu.SemaphoreType.DMA(shape)] * 2

    scratch = [
        vmem((slots + 1, tile, tile)), vmem((order, order)), vmem((order, order)),
        vmem((streams, row_size) + piece), vmem((streams, col_size) + piece), vmem((streams, row_size) + piece),
        vmem((streams,) + piece, F32), vmem((streams, x_size) + piece, F32), vmem((streams,) + piece, F32),
        *[vmem((streams, col_size) + piece)] * 4,
        *[vmem((streams,) + relay + piece)] * 2,
        *[vmem((streams, x_size) + piece)] * 4,
        pltpu.SemaphoreType.DMA,
        *sems(streams, x_size), *sems(streams, x_size),
        *sems(streams, col_size), *sems(streams, col_size),
        *sems(streams), *sems(streams, x_size),
        *sems(streams, x_size), *sems(streams, x_size),
        *sems(streams, col_size),
        *sems(streams, *relay), pltpu.SemaphoreType.DMA((streams,) + relay[::-1]),
    ]
    sizes = (row_size, col_size, blocks, tile, slots, streams)
    return pl.pallas_call(
        functools.partial(kernel, sizes),
        out_shape=jax.ShapeDtypeStruct((1, 1, piece_rows, vectors), F32),
        in_specs=[pl.BlockSpec(memory_space=pltpu.SMEM), pl.BlockSpec(memory_space=pltpu.VMEM),
                  pl.BlockSpec(memory_space=pl.ANY)],
        out_specs=pl.BlockSpec(memory_space=pltpu.VMEM),
        scratch_shapes=scratch,
        compiler_params=pltpu.CompilerParams(
            collective_id=0, has_side_effects=True, vmem_limit_bytes=56 * 1024 * 1024),
        cost_estimate=pl.CostEstimate(
            flops=6 * order * order * vectors, bytes_accessed=slots * tile * tile * 2, transcendentals=0),
    )(table, trial_panel, tile_values)


def solution(mesh):
    return jax.shard_map(
        per_device,
        mesh=mesh,
        in_specs=(
            P(("groups", "col"), "row", None, None),
            P(("groups", "row"), "col", None, None, None),
            P(("groups", "row"), "col", None),
            P(("groups", "row"), "col", None),
            P(("groups", "row"), "col"),
        ),
        out_specs=P(("groups", "row"), "col", None, None),
        check_vma=False,
    )
```

time: 94.3 us -> 87.2 us (0.925)
  Pallas kernels: 89.9 us -> 82.9 us
    pallas_call x1, Pallas kernels: 89.9 us -> 82.9 us  [per_device(): pl.pallas_call(functools.partial(kernel, sizes), out_shape=jax.ShapeDtype...]
where the time goes in v2:
time: 87.2 us; the launch traced here: 87 us
  Pallas kernels  82.9 us (95%)
  local copies, waits for them, and re-layouts  1.87 us (2%)
  other arithmetic  1.57 us (2%)
    pallas_call x1, Pallas kernels, per_device(): pl.pallas_call(functools.partial(kernel, sizes), out_shape=jax.ShapeDtype...  82.9 us
    unnamed x1, local copies, waits for them, and re-layouts  1.87 us

profile of v2, /device:TPU:0, one launch (start us, length us, event | category | flops | bytes accessed | tf_op | source)
XLA Modules:
  0.0 87.0 jit_solution(7746720761847273838)
XLA Ops:
  0.7 0.7 compare_select_fusion.3
  1.3 0.2 fusion.1
  1.5 0.1 select_reduce_fusion
  1.6 0.6 pad_add_fusion.slot_ref
  2.2 82.9 %shard_map.55 = f32[1,1,512,256]{3,2,1,0:T(8,128)} custom-call(s32[272]{0:T(512)} %pad_add_fusion.slot_ref, bf16[1,1,512,256]{3,2,1,0:T(8,128)(2,1)} %trial_ref.1, bf16[1,1,128,128,128]{4,3,2,1,0:T(8,128)(2,1)} %tiles_hbm.1), custom_call_target="tpu_custom_call" | custom-call | flops 6442450944 | bytes 4194304 | tf_op jit(solution)/shard_map/pallas_call | solution.py:358
  85.1 1.9 %copy.8 = f32[1,1,512,256]{3,2,1,0:T(8,128)} copy(f32[1,1,512,256]{3,2,1,0:T(8,128)} %shard_map.55) | data formatting | bytes 1048576
  (2 shorter events, 0.0 us)
